TPU v7x, 32 devices: a whole 2x2x4 slice. The times are simulated.
32 devices in a mesh: groups: 2 (over x), samples: 16 (over z, y, core).
Axes of the slice: x: 2, y: 2, z: 4, core: 2. Of those that a mesh axis runs over, the one named last changes fastest.
Arguments:
- energies: float32 [256, 393216], P(None, ('groups', 'samples')), parts along dimension 1, may hold values from -700 to 700
- mult: int32 [393216, 256], P(('groups', 'samples')), parts along dimension 0, may hold values from 0 to 3
- state_counts: int32 [512], P('groups'), parts along dimension 0, may hold values from 1 to 1536, 196608 in all
Outputs:
- free_energy: float32 [512, 256], P('groups'), parts along dimension 0
There are 2 independent parts, one for each index of `groups`. A program takes and returns all parts, laid end to end along the dimension named above; each array names one. Nothing has to cross between parts.
All inputs are finite; a program needn't handle non-finite values.
Results may differ from a plain program's by a relative error of at most 0.0003.
Values sent between devices are 32-bit elements; how exact they have to be, the bound alone decides.
A program may use at most 128 MiB of HBM per device.

v0:
```python
import jax
import jax.numpy as jnp
from jax import lax
from jax.sharding import PartitionSpec as P

ITERS = 4


def weighted_terms(boltz, weight, mult_part):
    denom = lax.dot_general(
        boltz, weight, (((0,), (0,)), ((), ())), preferred_element_type=jnp.float32
    )
    ratio = (mult_part.astype(jnp.float32) / denom).astype(jnp.bfloat16)
    return jnp.dot(boltz, ratio, preferred_element_type=jnp.float32)


def settle(partial_sums):
    totals = lax.psum(partial_sums, "samples")
    logs = jnp.log(totals)
    return logs[0:1] - logs


def on_device(energies, mult, state_counts):
    shift = jnp.min(energies, axis=0, keepdims=True)
    boltz = jnp.exp(shift - energies).astype(jnp.bfloat16)
    counts_f = state_counts.astype(jnp.float32)[:, None]
    num_states = energies.shape[0]
    num_reps = mult.shape[1]
    free = jnp.zeros((num_states, num_reps), jnp.float32)
    for step in range(ITERS):
        weight = (counts_f * jnp.exp(free)).astype(jnp.bfloat16)
        free = settle(weighted_terms(boltz, weight, mult))
    return free


def solution(mesh):
    in_specs = (P(None, ("groups", "samples")), P(("groups", "samples"), None), P("groups"))
    out_specs = P("groups", None)
    return jax.shard_map(
        on_device, mesh=mesh, in_specs=in_specs, out_specs=out_specs, check_vma=False
    )
```

profile of v0, /device:TPU:1, one launch (start us, length us, event | category | flops | bytes accessed | tf_op | source)
XLA Modules:
  0.0 444.2 jit_solution(2489789016998661210)
XLA Ops:
  6.5 0.0 all-reduce.5.cloned.1.call-start
  6.5 0.7 fusion.24
  7.2 5.2 %reduce_min.9 = f32[12288]{0:T(1024)S(1)} reduce(f32[256,12288]{1,0:T(8,128)} %param.3, f32[]{:T(128)} %constant.0.clone.1), dimensions={0}, to_apply=%region_0.0 | reduce | flops 3133440 | bytes 12632068 | tf_op jit(solution)/shard_map/reduce_min | solution.py:24
  12.4 9.0 %exponential_convert_fusion = bf16[256,12288]{1,0:T(8,128)(2,1)} fusion(f32[256,12288]{1,0:T(8,128)} %param.3, f32[12288]{0:T(1024)S(1)} %reduce_min.9), kind=kLoop, calls=%fused_computation.4 | loop fusion | flops 6291456 | bytes 18923520 | tf_op jit(solution)/shard_map/convert_element_type | solution.py:25
  21.4 12.6 %fusion = f32[256,256]{1,0:T(8,128)} fusion(bf16[256,12288]{1,0:T(8,128)(2,1)} %exponential_convert_fusion, s32[12288,256]{1,0:T(8,128)} %param.4, bf16[256]{0:T(256)(128)(2,1)S(1)} %get-tuple-element.6), kind=kOutput, calls=%fused_computation.5 | convolution fusion | flops 3230662656 | bytes 19137024 | tf_op jit(solution)/shard_map/dot_general | solution.py:14
  34.0 0.0 all-reduce.5.cloned.1.call-update
  34.0 0.0 all-reduce.7.cloned.1.call-start
  34.0 91.6 %all-reduce.5.cloned.1.call-done = f32[256,256]{1,0:T(8,128)} async-done(((f32[256,256]{1,0:T(8,128)}), f32[256,256]{1,0:T(8,128)}) %all-reduce.5.cloned.1.call-update) | async-done | bytes 262160 | tf_op jit(solution)/shard_map/psum | solution.py:18
  125.6 1.0 log.12
  126.6 12.7 %fusion.1 = f32[256,256]{1,0:T(8,128)} fusion(bf16[256,12288]{1,0:T(8,128)(2,1)} %exponential_convert_fusion, s32[12288,256]{1,0:T(8,128)} %param.4, f32[256]{0:T(256)S(1)} %bitcast.14, f32[256]{0:T(256)S(1)} %get-tuple-element.5, f32[256,256]{1,0:T(8,128)} %all-reduce.5.cloned.1.call-done), kind=kOutput, calls=%fused_computation.6 | convolution fusion | flops 3230859264 | bytes 19400704 | tf_op jit(solution)/shard_map/dot_general | solution.py:14
  139.3 0.0 all-reduce.7.cloned.1.call-update
  139.3 0.2 all-reduce.9.cloned.1.call-start
  139.5 89.2 %all-reduce.7.cloned.1.call-done = f32[256,256]{1,0:T(8,128)} async-done(((f32[256,256]{1,0:T(8,128)}), f32[256,256]{1,0:T(8,128)}) %all-reduce.7.cloned.1.call-update) | async-done | bytes 262160 | tf_op jit(solution)/shard_map/psum | solution.py:18
  228.7 1.0 log.13
  229.7 12.7 %fusion.2 = f32[256,256]{1,0:T(8,128)} fusion(bf16[256,12288]{1,0:T(8,128)(2,1)} %exponential_convert_fusion, s32[12288,256]{1,0:T(8,128)} %param.4, f32[256]{0:T(256)S(1)} %bitcast.15, f32[256]{0:T(256)S(1)} %get-tuple-element.5, f32[256,256]{1,0:T(8,128)} %all-reduce.7.cloned.1.call-done), kind=kOutput, calls=%fused_computation.7 | convolution fusion | flops 3230859264 | bytes 19400704 | tf_op jit(solution)/shard_map/dot_general | solution.py:14
  242.4 0.0 all-reduce.9.cloned.1.call-update
  242.4 0.0 all-reduce.11.cloned.1.call-start
  242.5 89.4 %all-reduce.9.cloned.1.call-done = f32[256,256]{1,0:T(8,128)} async-done(((f32[256,256]{1,0:T(8,128)}), f32[256,256]{1,0:T(8,128)}) %all-reduce.9.cloned.1.call-update) | async-done | bytes 262160 | tf_op jit(solution)/shard_map/psum | solution.py:18
  331.8 1.0 log.14
  332.8 12.7 %fusion.3 = f32[256,256]{1,0:T(8,128)} fusion(bf16[256,12288]{1,0:T(8,128)(2,1)} %exponential_convert_fusion, s32[12288,256]{1,0:T(8,128)} %param.4, f32[256]{0:T(256)S(1)} %bitcast.13, f32[256]{0:T(256)S(1)} %get-tuple-element.5, f32[256,256]{1,0:T(8,128)} %all-reduce.9.cloned.1.call-done), kind=kOutput, calls=%fused_computation.8 | convolution fusion | flops 3230859264 | bytes 19400704 | tf_op jit(solution)/shard_map/dot_general | solution.py:14
  345.5 0.0 all-reduce.11.cloned.1.call-update
  345.5 89.4 %all-reduce.11.cloned.1.call-done = f32[256,256]{1,0:T(8,128)} async-done(((f32[256,256]{1,0:T(8,128)}), f32[256,256]{1,0:T(8,128)}) %all-reduce.11.cloned.1.call-update) | async-done | bytes 262160 | tf_op jit(solution)/shard_map/psum | solution.py:18
  435.0 1.0 log.15
  436.0 1.7 broadcast_subtract_fusion
  (4 shorter events, 0.0 us)
Async XLA Ops:
  6.5 119.1 %all-reduce.5.cloned.1.call-start = ((), (), s32[]{:S(2)}) async-start(), calls=%async_computation | async-start | bytes 524288 | tf_op jit(solution)/shard_map/psum | solution.py:18
  34.0 194.7 %all-reduce.7.cloned.1.call-start = ((), (), s32[]{:S(2)}) async-start(), calls=%async_computation.1 | async-start | bytes 524288 | tf_op jit(solution)/shard_map/psum | solution.py:18
  139.3 192.5 %all-reduce.9.cloned.1.call-start = ((), (), s32[]{:S(2)}) async-start(), calls=%async_computation.2 | async-start | bytes 524288 | tf_op jit(solution)/shard_map/psum | solution.py:18
  242.4 192.5 %all-reduce.11.cloned.1.call-start = ((), (), s32[]{:S(2)}) async-start(), calls=%async_computation.3 | async-start | bytes 524288 | tf_op jit(solution)/shard_map/psum | solution.py:18
Sparse Core Ops, SparseCore 0:
  34.1 91.4 all-reduce.4
  139.4 89.2 all-reduce.6
  242.5 89.2 all-reduce.8
  345.6 89.2 all-reduce.10
where the time goes:
time: 445 us; the launch traced here: 444 us
  waiting for transfers between devices  360 us (81%)
  matrix products  50.5 us (11%)
  other arithmetic  16.5 us (4%)
  between operations  13.2 us (3%)
    psum x4, waiting for transfers between devices, settle(): totals = lax.psum(partial_sums, 'samples')  360 us
    dot_general x4, matrix products, weighted_terms(): return jnp.dot(boltz, ratio, preferred_element_type=jnp.float32)  50.5 us
    convert_element_type x1, other arithmetic, on_device(): boltz = jnp.exp(shift - energies).astype(jnp.bfloat16)  8.95 us
  transfers between devices with their start and end apart: 4, of which 4 were waited for; matrix products, arithmetic and copies ran while one was open for 0% of the time, Pallas kernels for 0%

commit v1 on v0

--- a/solution.py
+++ b/solution.py
@@ -15,7 +15,8 @@
 
 
 def settle(partial_sums):
-    totals = lax.psum(partial_sums, "samples")
+    pieces = lax.all_gather(partial_sums, "samples", axis=0, tiled=False)
+    totals = pieces.sum(axis=0)
     logs = jnp.log(totals)
     return logs[0:1] - logs
 

time: 445 us -> 291 us (0.65)
  waiting for transfers between devices: 360 us -> 201 us
  other arithmetic: 16.5 us -> 25.5 us
    psum x4 -> x0, waiting for transfers between devices: 360 us -> none  [settle(): totals = lax.psum(partial_sums, 'samples')]
    all_gather x0 -> x4, waiting for transfers between devices: none -> 201 us  [settle(): pieces = lax.all_gather(partial_sums, 'samples', axis=0, tiled=False)]
    reduce_sum x0 -> x4, other arithmetic: none -> 9.9 us  [settle(): totals = pieces.sum(axis=0)]
where the time goes in v1:
time: 291 us; the launch traced here: 290 us
  waiting for transfers between devices  201 us (69%)
  matrix products  50.3 us (17%)
  other arithmetic  25.5 us (9%)
  between operations  13.2 us (5%)
    all_gather x4, waiting for transfers between devices, settle(): pieces = lax.all_gather(partial_sums, 'samples', axis=0, tiled=False)  201 us
    dot_general x4, matrix products, weighted_terms(): return jnp.dot(boltz, ratio, preferred_element_type=jnp.float32)  50.3 us
    reduce_sum x4, other arithmetic, settle(): totals = pieces.sum(axis=0)  9.9 us
    convert_element_type x1, other arithmetic, on_device(): boltz = jnp.exp(shift - energies).astype(jnp.bfloat16)  8.95 us
  transfers between devices with their start and end apart: 4, of which 4 were waited for; matrix products, arithmetic and copies ran while one was open for 0% of the time, Pallas kernels for 0%

profile of v1, /device:TPU:1, one launch (start us, length us, event | category | flops | bytes accessed | tf_op | source)
XLA Modules:
  0.0 290.1 jit_solution(13230520642509794378)
XLA Ops:
  6.5 0.0 all-gather.9.cloned.1.call-start
  6.5 0.7 fusion.24
  7.2 5.2 %reduce_min.9 = f32[12288]{0:T(1024)S(1)} reduce(f32[256,12288]{1,0:T(8,128)} %param.3, f32[]{:T(128)} %constant.0.clone.1), dimensions={0}, to_apply=%region_0.0 | reduce | flops 3133440 | bytes 12632068 | tf_op jit(solution)/shard_map/reduce_min | solution.py:25
  12.4 9.0 %exponential_convert_fusion = bf16[256,12288]{1,0:T(8,128)(2,1)} fusion(f32[256,12288]{1,0:T(8,128)} %param.3, f32[12288]{0:T(1024)S(1)} %reduce_min.9), kind=kLoop, calls=%fused_computation.4 | loop fusion | flops 6291456 | bytes 18923520 | tf_op jit(solution)/shard_map/convert_element_type | solution.py:26
  21.4 12.6 %fusion = f32[256,256]{1,0:T(8,128)} fusion(bf16[256,12288]{1,0:T(8,128)(2,1)} %exponential_convert_fusion, s32[12288,256]{1,0:T(8,128)} %param.4, bf16[256]{0:T(256)(128)(2,1)S(1)} %get-tuple-element.6), kind=kOutput, calls=%fused_computation.5 | convolution fusion | flops 3230662656 | bytes 19137024 | tf_op jit(solution)/shard_map/dot_general | solution.py:14
  34.0 0.0 all-gather.9.cloned.1.call-update
  34.0 0.0 all-gather.11.cloned.1.call-start
  34.0 53.2 %all-gather.9.cloned.1.call-done = f32[4096,256]{1,0:T(8,128)} async-done(((f32[256,256]{1,0:T(8,128)}), f32[4096,256]{1,0:T(8,128)}) %all-gather.9.cloned.1.call-update) | async-done | bytes 4194320 | tf_op jit(solution)/shard_map/all_gather | solution.py:18
  87.2 2.5 reduce_sum.36
  89.7 12.6 %fusion.1 = f32[256,256]{1,0:T(8,128)} fusion(bf16[256,12288]{1,0:T(8,128)(2,1)} %exponential_convert_fusion, s32[12288,256]{1,0:T(8,128)} %param.4, f32[256]{0:T(256)S(1)} %bitcast.22, f32[256]{0:T(256)S(1)} %get-tuple-element.5, f32[256,256]{1,0:T(8,128)S(1)} %reduce_sum.36), kind=kOutput, calls=%fused_computation.6 | convolution fusion | flops 3230859264 | bytes 19400704 | tf_op jit(solution)/shard_map/dot_general | solution.py:14
  102.3 0.0 all-gather.11.cloned.1.call-update
  102.3 0.2 all-gather.13.cloned.1.call-start
  102.6 49.0 %all-gather.11.cloned.1.call-done = f32[4096,256]{1,0:T(8,128)} async-done(((f32[256,256]{1,0:T(8,128)}), f32[4096,256]{1,0:T(8,128)}) %all-gather.11.cloned.1.call-update) | async-done | bytes 4194320 | tf_op jit(solution)/shard_map/all_gather | solution.py:18
  151.6 2.5 reduce_sum.37
  154.1 12.6 %fusion.2 = f32[256,256]{1,0:T(8,128)} fusion(bf16[256,12288]{1,0:T(8,128)(2,1)} %exponential_convert_fusion, s32[12288,256]{1,0:T(8,128)} %param.4, f32[256]{0:T(256)S(1)} %bitcast.23, f32[256]{0:T(256)S(1)} %get-tuple-element.5, f32[256,256]{1,0:T(8,128)S(1)} %reduce_sum.37), kind=kOutput, calls=%fused_computation.7 | convolution fusion | flops 3230859264 | bytes 19400704 | tf_op jit(solution)/shard_map/dot_general | solution.py:14
  166.7 0.0 all-gather.13.cloned.1.call-update
  166.7 0.0 all-gather.15.cloned.1.call-start
  166.8 49.2 %all-gather.13.cloned.1.call-done = f32[4096,256]{1,0:T(8,128)} async-done(((f32[256,256]{1,0:T(8,128)}), f32[4096,256]{1,0:T(8,128)}) %all-gather.13.cloned.1.call-update) | async-done | bytes 4194320 | tf_op jit(solution)/shard_map/all_gather | solution.py:18
  215.9 2.5 reduce_sum.38
  218.5 12.6 %fusion.3 = f32[256,256]{1,0:T(8,128)} fusion(bf16[256,12288]{1,0:T(8,128)(2,1)} %exponential_convert_fusion, s32[12288,256]{1,0:T(8,128)} %param.4, f32[256]{0:T(256)S(1)} %bitcast.21, f32[256]{0:T(256)S(1)} %get-tuple-element.5, f32[256,256]{1,0:T(8,128)S(1)} %reduce_sum.38), kind=kOutput, calls=%fused_computation.8 | convolution fusion | flops 3230859264 | bytes 19400704 | tf_op jit(solution)/shard_map/dot_general | solution.py:14
  231.0 0.0 all-gather.15.cloned.1.call-update
  231.1 49.2 %all-gather.15.cloned.1.call-done = f32[4096,256]{1,0:T(8,128)} async-done(((f32[256,256]{1,0:T(8,128)}), f32[4096,256]{1,0:T(8,128)}) %all-gather.15.cloned.1.call-update) | async-done | bytes 4194320 | tf_op jit(solution)/shard_map/all_gather | solution.py:18
  280.3 2.5 reduce_sum.39
  282.8 0.7 broadcast_subtract_fusion
  (8 shorter events, 0.2 us)
Async XLA Ops:
  6.5 80.7 %all-gather.9.cloned.1.call-start = ((), (), s32[]{:S(2)}) async-start(), calls=%async_computation | async-start | bytes 4456448 | tf_op jit(solution)/shard_map/all_gather | solution.py:18
  34.0 117.6 %all-gather.11.cloned.1.call-start = ((), (), s32[]{:S(2)}) async-start(), calls=%async_computation.1 | async-start | bytes 4456448 | tf_op jit(solution)/shard_map/all_gather | solution.py:18
  102.3 113.6 %all-gather.13.cloned.1.call-start = ((), (), s32[]{:S(2)}) async-start(), calls=%async_computation.2 | async-start | bytes 4456448 | tf_op jit(solution)/shard_map/all_gather | solution.py:18
  166.7 113.6 %all-gather.15.cloned.1.call-start = ((), (), s32[]{:S(2)}) async-start(), calls=%async_computation.3 | async-start | bytes 4456448 | tf_op jit(solution)/shard_map/all_gather | solution.py:18
Sparse Core Ops, SparseCore 0:
  34.1 53.0 all-gather.8
  102.5 49.0 all-gather.10
  166.8 49.0 all-gather.12
  231.2 49.0 all-gather.14
